TPU v7x, 512 devices: a whole 4x8x8 slice. The times are simulated.
512 devices in a mesh: dp: 16 (over y, core), mp: 32 (over x, z).
Axes of the slice: x: 4, y: 8, z: 8, core: 2. Of those that a mesh axis runs over, the one named last changes fastest.
Arguments:
- gate_proj: bfloat16 [14336, 8192], P('mp', 'dp'), may hold values from -0.0625 to 0.0625
- up_proj: bfloat16 [14336, 8192], P('mp', 'dp'), may hold values from -0.0625 to 0.0625
- down_proj: bfloat16 [8192, 14336], P('dp', 'mp'), may hold values from -0.25 to 0.25
- partition: int32 [14336], replicated, may hold values from 0 to 14335, as said below
- tokens: bfloat16 [32768, 8192], P('mp', 'dp'), may hold values from -6 to 6
- targets: bfloat16 [32768, 8192], P('mp', 'dp'), may hold values from -3 to 3
- routes: int32 [32768, 1], P('mp'), may hold values from 0 to 31; in each aligned block of 1024 rows (0 to 1023, 1024 to 2047, ...) at most 42 rows name the same one
- combine: bfloat16 [32768], P('mp'), may hold values from 0.19921875 to 1
Outputs:
- down_grad: float32 [32, 448, 8192], P('mp', None, 'dp')
Inputs may be any that keep to these rules, and one draw needn't show every extreme that they name: partition is a permutation of 0 to 14335. Of the 448 hidden units n in rows s * 448 to (s + 1) * 448 - 1 of one tensor shard s, at most 21 belong to one expert, and some shard gives exactly 21 to some expert. `routes`: of the 1024 tokens of one index of mp, at most 42 name the same expert, a bound that some block reaches of them.
All inputs are finite; a program needn't handle non-finite values.
Results may differ from a plain program's by a relative error of at most 0.0041.
Values may be sent and summed in bfloat16 or wider, within the bound.
A program may use at most 64 MiB of HBM per device.

v0:
```python
import jax
import jax.numpy as jnp
from jax import lax
from jax.sharding import PartitionSpec as P


def hidden_units(sums):
    return (jax.nn.silu(sums[:, 0]) * sums[:, 1]).astype(jnp.bfloat16)


def ranks_of(onehot):
    count = onehot.shape[0]
    order = jnp.arange(count, dtype=jnp.int32)
    lower = (order[:, None] >= order[None, :]).astype(jnp.bfloat16)
    running = jnp.dot(lower, onehot, preferred_element_type=jnp.float32)
    return (jnp.sum(running * onehot.astype(jnp.float32), axis=1) - 1.0).astype(jnp.int32)


def sources_of(slot_id, slot_total, count):
    slot_range = jnp.arange(slot_total, dtype=jnp.int32)
    item_ids = jnp.arange(count, dtype=jnp.int32)
    matched = jnp.sum(
        jnp.where(slot_id[None, :] == slot_range[:, None], item_ids[None, :] + 1, 0), axis=1
    )
    return jnp.where(matched > 0, matched - 1, count)


def local(gate_proj, up_proj, down_proj, partition, tokens, targets, routes, combine):
    experts = lax.axis_size("mp")
    neurons = gate_proj.shape[0]
    columns = gate_proj.shape[1]
    own_index = lax.axis_index("mp")
    average = neurons // experts
    neuron_cap = average + average // 2
    expert_ids = jnp.arange(experts, dtype=jnp.int32)
    neuron_ids = jnp.arange(neurons, dtype=jnp.int32)
    all_owner = (partition // neurons).reshape(experts, neurons)
    all_place = (partition % neurons).reshape(experts, neurons)
    owner_here = lax.dynamic_index_in_dim(all_owner, own_index, 0, keepdims=False)
    member_here = (owner_here[:, None] == expert_ids[None, :]).astype(jnp.bfloat16)
    rank_here = ranks_of(member_here)
    neuron_source = sources_of(owner_here * neuron_cap + rank_here, experts * neuron_cap, neurons)
    stacked = jnp.concatenate([gate_proj, up_proj, down_proj.T], axis=1)
    outgoing = jnp.take(stacked, neuron_source, axis=0, mode="fill", fill_value=0).reshape(
        experts, neuron_cap, 3 * columns
    )
    arrived = lax.all_to_all(outgoing, "mp", split_axis=0, concat_axis=0, tiled=True)
    mine = all_owner == own_index
    upper = (neuron_ids[:, None] <= neuron_ids[None, :]).astype(jnp.bfloat16)
    running = jnp.dot(mine.astype(jnp.bfloat16), upper, preferred_element_type=jnp.float32)
    rank_recv = running.astype(jnp.int32) - 1
    cap_ids = jnp.arange(neuron_cap, dtype=jnp.int32)
    landing = mine[:, :, None] & (rank_recv[:, :, None] == cap_ids[None, None, :])
    slot_place = (jnp.sum(jnp.where(landing, all_place[:, :, None] + 1, 0), axis=1) - 1).reshape(-1)
    arrival_ids = jnp.arange(experts * neuron_cap, dtype=jnp.int32)
    slot_of_place = jnp.sum(
        jnp.where(slot_place[None, :] == neuron_ids[:, None], arrival_ids[None, :], 0), axis=1
    )
    weights = jnp.take(arrived.reshape(experts * neuron_cap, 3 * columns), slot_of_place, axis=0)
    gate_up = weights[:, : 2 * columns].reshape(neurons, 2, columns)
    down_rows = weights[:, 2 * columns :]
    tok_count = tokens.shape[0]
    portion = tok_count // experts
    capacity = portion + max(1, portion // 3)
    chosen = routes[:, 0]
    picked = (chosen[:, None] == expert_ids[None, :]).astype(jnp.bfloat16)
    slot_index = ranks_of(picked)
    token_source = sources_of(chosen * capacity + slot_index, experts * capacity, tok_count)
    send_rows = jnp.take(tokens, token_source, axis=0, mode="fill", fill_value=0).reshape(
        experts, capacity, columns
    )
    send_goal = jnp.take(targets, token_source, axis=0, mode="fill", fill_value=0).reshape(
        experts, capacity, columns
    )
    send_weight = jnp.take(combine, token_source, axis=0, mode="fill", fill_value=0).reshape(
        experts, capacity
    )
    rows_in, goal_in, weight_in = (
        lax.all_to_all(send_rows, "mp", split_axis=0, concat_axis=0, tiled=True),
        lax.all_to_all(send_goal, "mp", split_axis=0, concat_axis=0, tiled=True),
        lax.all_to_all(send_weight, "mp", split_axis=0, concat_axis=0, tiled=True),
    )
    slot_count = experts * capacity
    rows_in = rows_in.reshape(slot_count, columns)
    goal_in = goal_in.reshape(slot_count, columns)
    weight_in = weight_in.reshape(slot_count)
    partial_value = jnp.einsum("sc,jkc->skj", rows_in, gate_up, preferred_element_type=jnp.float32)
    scale = tok_count ** (-0.5)
    totals = lax.psum(partial_value, "dp")
    piece = hidden_units(totals)
    produced = jnp.dot(piece, down_rows, preferred_element_type=jnp.float32)
    goal = goal_in.astype(jnp.float32)
    weight = weight_in.astype(jnp.float32)[:, None]
    delta = (weight * (weight * produced - goal) * scale).astype(jnp.bfloat16)
    gradient = lax.dot_general(
        piece, delta, (((0,), (0,)), ((), ())), preferred_element_type=jnp.float32
    )
    return gradient[None]


def solution(mesh):
    in_specs = (
        P("mp", "dp"),
        P("mp", "dp"),
        P("dp", "mp"),
        P(),
        P("mp", "dp"),
        P("mp", "dp"),
        P("mp", None),
        P("mp"),
    )
    out_specs = P("mp", None, "dp")
    return jax.shard_map(local, mesh=mesh, in_specs=in_specs, out_specs=out_specs, check_vma=False)
```

profile of v0, /device:TPU:25, one launch (start us, length us, event | category | flops | bytes accessed | tf_op | source)
XLA Modules:
  0.0 315.5 jit_solution(5437780581741791936)
XLA Ops:
  6.5 0.0 copy-start
  6.5 1.3 fusion.9
  7.9 0.7 iota_add_fusion
  8.6 0.6 select_reduce_fusion
  9.3 0.0 copy-done
  9.3 0.0 copy-start.2
  9.3 5.3 %gather_fusion.3 = bf16[1344,512]{1,0:T(8,128)(2,1)} fusion(bf16[1024,512]{1,0:T(8,128)(2,1)S(1)} %copy-done, s32[2048]{0:T(1024)S(1)} %pad_clamp_fusion.1), kind=kCustom, calls=%fused_computation.clone | custom fusion | bytes 2757888 | tf_op jit(solution)/shard_map/jit(_take)/gather | solution.py:69
  14.6 0.0 copy-done.2
  14.6 5.3 %gather_fusion.4 = bf16[1344,512]{1,0:T(8,128)(2,1)} fusion(bf16[1024,512]{1,0:T(8,128)(2,1)S(1)} %copy-done.2, s32[2048]{0:T(1024)S(1)} %pad_clamp_fusion.1), kind=kCustom, calls=%fused_computation.1.clone | custom fusion | bytes 2757888 | tf_op jit(solution)/shard_map/jit(_take)/gather | solution.py:72
  19.9 3.1 broadcast_select_fusion.3
  23.1 1.3 reshape.253
  24.4 0.0 copy-start.7
  24.4 0.0 copy-start.5
  24.4 0.0 copy-start.6
  24.4 13.1 %all-to-all-start.1 = ((bf16[32,42,512]{2,1,0:T(8,128)(2,1)}), bf16[32,42,512]{2,1,0:T(8,128)(2,1)}, u32[]{:S(2)}, u32[]{:S(2)}) async-start(bf16[32,42,512]{2,1,0:T(8,128)(2,1)} %reshape.253), calls=%async_computation.1 | async-start | bytes 3145728 | tf_op jit(solution)/shard_map/all_to_all | solution.py:79
  37.6 0.0 copy-done.7
  37.6 0.7 fusion.21
  38.3 0.1 reshape.250
  38.4 0.2 fusion.11
  38.7 0.2 select_reduce_fusion.1
  38.9 0.1 select_n.171
  39.0 0.0 copy-done.5
  39.1 0.0 copy-done.6
  39.1 1.1 pad_maximum_fusion
  40.2 3.7 %gather_fusion = bf16[672,1536]{1,0:T(8,128)(2,1)} fusion(bf16[448,1536]{1,0:T(8,128)(2,1)S(1)} %pad_maximum_fusion, s32[1024]{0:T(1024)S(1)} %pad_clamp_fusion.3), kind=kCustom, calls=%fused_computation.2 | custom fusion | bytes 4131456 | tf_op jit(solution)/shard_map/jit(_take)/gather | solution.py:44
  43.9 2.7 gather.20
  46.6 1.6 broadcast_select_fusion
  48.2 26.2 %all-to-all-done.1 = bf16[32,42,512]{2,1,0:T(8,128)(2,1)} async-done(((bf16[32,42,512]{2,1,0:T(8,128)(2,1)}), bf16[32,42,512]{2,1,0:T(8,128)(2,1)}, u32[]{:S(2)}, u32[]{:S(2)}) %all-to-all-start.1) | async-done | bytes 1376288 | tf_op jit(solution)/shard_map/all_to_all | solution.py:79
  74.4 7.6 %all-to-all-start = ((bf16[32,21,1536]{2,1,0:T(8,128)(2,1)}), bf16[32,21,1536]{2,1,0:T(8,128)(2,1)S(1)}, u32[]{:S(2)}, u32[]{:S(2)}) async-start(bf16[32,21,1536]{2,1,0:T(8,128)(2,1)} %broadcast_select_fusion), calls=%async_computation | async-start | bytes 4718592 | tf_op jit(solution)/shard_map/all_to_all | solution.py:47
  82.0 0.9 add.188
  82.9 0.2 fusion.10
  83.1 0.5 select_reduce_fusion.3
  83.6 0.0 copy-start.1
  83.6 0.1 copy.12
  83.7 0.1 sub.38
  83.8 3.3 %reshape.255 = bf16[32,42,512]{2,1,0:T(8,128)(2,1)} reshape(bf16[1344,512]{1,0:T(8,128)(2,1)} %get-tuple-element.11) | data formatting | bytes 2752512 | tf_op jit(solution)/shard_map/reshape | solution.py:72
  87.1 0.1 select_n.180
  87.2 0.0 copy-done.1
  87.3 8.4 %gather_fusion.2 = bf16[1344]{0:T(1024)(128)(2,1)S(1)} fusion(bf16[1024]{0:T(1024)(128)(2,1)S(1)} %copy-done.1, s32[2048]{0:T(1024)S(1)} %pad_clamp_fusion), kind=kCustom, calls=%fused_computation.4 | custom fusion | bytes 10752 | tf_op jit(solution)/shard_map/jit(_take)/gather | solution.py:75
  95.7 0.1 gather.23
  95.8 0.6 copy.14
  96.4 0.2 select_reduce_fusion.2
  96.7 3.4 %reshape.304 = bf16[1344,512,1]{1,0,2:T(8,128)(2,1)} reshape(bf16[32,42,512]{2,1,0:T(8,128)(2,1)} %all-to-all-done.1) | data formatting | bytes 2752512 | tf_op jit(solution)/shard_map/reshape | solution.py:84
  100.0 36.5 %all-to-all-done = bf16[32,21,1536]{2,1,0:T(8,128)(2,1)S(1)} async-done(((bf16[32,21,1536]{2,1,0:T(8,128)(2,1)}), bf16[32,21,1536]{2,1,0:T(8,128)(2,1)S(1)}, u32[]{:S(2)}, u32[]{:S(2)}) %all-to-all-start) | async-done | bytes 2064416 | tf_op jit(solution)/shard_map/all_to_all | solution.py:47
  136.5 0.0 copy-start.3
  136.5 1.4 copy-done.3
  137.9 6.9 %all-to-all-start.2 = ((bf16[32,1,42]{2,1,0:T(2,128)(2,1)}), bf16[32,1,42]{2,1,0:T(2,128)(2,1)S(1)}, u32[]{:S(2)}, u32[]{:S(2)}) async-start(bf16[32,1,42]{2,1,0:T(2,128)(2,1)} %copy.14), calls=%async_computation.2 | async-start | bytes 32768 | tf_op jit(solution)/shard_map/all_to_all | solution.py:81
  144.8 2.7 reshape.251
  147.6 2.9 gather_fusion.1
  150.5 1.5 broadcast_select_fusion.1
  152.0 0.0 copy-start.4
  152.0 1.1 copy-done.4
  153.1 0.1 slice.26
  153.2 0.2 all-to-all-done.2
  153.4 9.0 %all-to-all-start.3 = ((bf16[32,42,512]{2,1,0:T(8,128)(2,1)}), bf16[32,42,512]{2,1,0:T(8,128)(2,1)S(1)}, u32[]{:S(2)}, u32[]{:S(2)}) async-start(bf16[32,42,512]{2,1,0:T(8,128)(2,1)} %reshape.255), calls=%async_computation.3 | async-start | bytes 3145728 | tf_op jit(solution)/shard_map/all_to_all | solution.py:80
  162.5 0.2 all-reduce.2.cloned.1.call-start
  162.7 5.2 %convolution_bitcast_fusion = f32[1344,2,448]{0,2,1:T(8,128)} fusion(bf16[1344,512,1]{1,0,2:T(8,128)(2,1)} %reshape.304, bf16[56,2,8,512]{3,2,1,0:T(8,128)(2,1)S(1)} %bitcast.31), kind=kOutput, calls=%fused_computation.9 | convolution fusion | flops 1233125376 | bytes 7110656 | tf_op jit(solution)/shard_map/sc,jkc->skj/dot_general | solution.py:87
  167.9 0.0 all-reduce.2.cloned.1.call-update
  168.0 0.1 convert_reduce_fusion
  168.0 0.1 reshape.256
  168.1 31.0 %all-to-all-done.3 = bf16[32,42,512]{2,1,0:T(8,128)(2,1)S(1)} async-done(((bf16[32,42,512]{2,1,0:T(8,128)(2,1)}), bf16[32,42,512]{2,1,0:T(8,128)(2,1)S(1)}, u32[]{:S(2)}, u32[]{:S(2)}) %all-to-all-start.3) | async-done | bytes 1376288 | tf_op jit(solution)/shard_map/all_to_all | solution.py:80
  199.1 1.7 reshape.257
  200.8 100.0 %all-reduce.2.cloned.1.call-done = f32[1344,2,448]{0,2,1:T(8,128)} async-done(((f32[1344,2,448]{0,2,1:T(8,128)}), f32[1344,2,448]{0,2,1:T(8,128)}) %all-reduce.2.cloned.1.call-update) | async-done | bytes 4816912 | tf_op jit(solution)/shard_map/psum | solution.py:89
  300.8 7.9 %convolution_bitcast_fusion.1 = f32[1,448,512]{2,1,0:T(8,128)} fusion(f32[1344,512]{1,0:T(8,128)} %reshape.257, f32[1344]{0:T(1024)S(1)} %reshape.256, f32[1344,2,448]{0,2,1:T(8,128)} %all-reduce.2.cloned.1.call-done, bf16[448,1536]{1,0:T(8,128)(2,1)} %copy-done.4), kind=kOutput, calls=%fused_computation.31 | convolution fusion | flops 1243791360 | bytes 14226688 | tf_op jit(solution)/shard_map/dot_general | solution.py:95
  (19 shorter events, 0.2 us)
Async XLA Ops:
  6.5 2.7 copy-start
  9.3 5.4 %copy-start.2 = (bf16[1024,512]{1,0:T(8,128)(2,1)S(1)}, bf16[1024,512]{1,0:T(8,128)(2,1)}, u32[]{:S(2)}) copy-start(bf16[1024,512]{1,0:T(8,128)(2,1)} %param.15) | copy-start | bytes 3145732
  24.4 13.2 %copy-start.7 = (s32[14336]{0:T(1024)S(1)}, s32[14336]{0:T(1024)}, u32[]{:S(2)}) copy-start(s32[14336]{0:T(1024)} %param.13) | copy-start | bytes 172036
  24.4 14.6 %copy-start.5 = (bf16[512,448]{0,1:T(8,128)(2,1)S(1)}, bf16[512,448]{0,1:T(8,128)(2,1)}, u32[]{:S(2)}) copy-start(bf16[512,448]{0,1:T(8,128)(2,1)} %param.12) | copy-start | bytes 1376260
  24.4 14.6 %copy-start.6 = (bf16[448,512]{1,0:T(8,128)(2,1)S(1)}, bf16[448,512]{1,0:T(8,128)(2,1)}, u32[]{:S(2)}) copy-start(bf16[448,512]{1,0:T(8,128)(2,1)} %param.11) | copy-start | bytes 1376260
  24.4 49.9 %all-to-all-start.1 = ((bf16[32,42,512]{2,1,0:T(8,128)(2,1)}), bf16[32,42,512]{2,1,0:T(8,128)(2,1)}, u32[]{:S(2)}, u32[]{:S(2)}) async-start(bf16[32,42,512]{2,1,0:T(8,128)(2,1)} %reshape.253), calls=%async_computation.1 | async-start | bytes 3145728 | tf_op jit(solution)/shard_map/all_to_all | solution.py:79
  74.4 62.1 %all-to-all-start = ((bf16[32,21,1536]{2,1,0:T(8,128)(2,1)}), bf16[32,21,1536]{2,1,0:T(8,128)(2,1)S(1)}, u32[]{:S(2)}, u32[]{:S(2)}) async-start(bf16[32,21,1536]{2,1,0:T(8,128)(2,1)} %broadcast_select_fusion), calls=%async_computation | async-start | bytes 4718592 | tf_op jit(solution)/shard_map/all_to_all | solution.py:47
  83.6 3.7 %copy-start.1 = (bf16[1024]{0:T(1024)(128)(2,1)S(1)}, bf16[1024]{0:T(1024)(128)(2,1)}, u32[]{:S(2)}) copy-start(bf16[1024]{0:T(1024)(128)(2,1)} %param.17) | copy-start | bytes 6148
  136.5 1.4 copy-start.3
  137.9 15.5 %all-to-all-start.2 = ((bf16[32,1,42]{2,1,0:T(2,128)(2,1)}), bf16[32,1,42]{2,1,0:T(2,128)(2,1)S(1)}, u32[]{:S(2)}, u32[]{:S(2)}) async-start(bf16[32,1,42]{2,1,0:T(2,128)(2,1)} %copy.14), calls=%async_computation.2 | async-start | bytes 32768 | tf_op jit(solution)/shard_map/all_to_all | solution.py:81
  152.0 1.1 copy-start.4
  153.4 45.7 %all-to-all-start.3 = ((bf16[32,42,512]{2,1,0:T(8,128)(2,1)}), bf16[32,42,512]{2,1,0:T(8,128)(2,1)S(1)}, u32[]{:S(2)}, u32[]{:S(2)}) async-start(bf16[32,42,512]{2,1,0:T(8,128)(2,1)} %reshape.255), calls=%async_computation.3 | async-start | bytes 3145728 | tf_op jit(solution)/shard_map/all_to_all | solution.py:80
  162.5 138.3 %all-reduce.2.cloned.1.call-start = ((), (), s32[]{:S(2)}) async-start(), calls=%async_computation.4 | async-start | bytes 10092544 | tf_op jit(solution)/shard_map/psum | solution.py:89
Sparse Core Ops, SparseCore 0:
  168.1 132.6 all-reduce.1
where the time goes:
time: 316 us; the launch traced here: 315 us
  waiting for transfers between devices  194 us (61%)
  local copies, waits for them, and re-layouts  45.6 us (14%)
  starting transfers between devices  36.9 us (12%)
  matrix products  14.8 us (5%)
  between operations  13.7 us (4%)
  other arithmetic  10.6 us (3%)
    psum x1, waiting for transfers between devices, local(): totals = lax.psum(partial_value, 'dp')  100 us
    all_to_all x1, waiting for transfers between devices, local(): lax.all_to_all(outgoing, 'mp', split_axis=0, concat_axis=0, tiled=True)  36.5 us
    all_to_all x1, waiting for transfers between devices, local(): lax.all_to_all(send_goal, 'mp', split_axis=0, concat_axis=0, tiled=True)  31 us
    all_to_all x1, waiting for transfers between devices, local(): lax.all_to_all(send_rows, 'mp', split_axis=0, concat_axis=0, tiled=True)  26.2 us
    all_to_all x1, starting transfers between devices, local(): lax.all_to_all(send_rows, 'mp', split_axis=0, concat_axis=0, tiled=True)  13.1 us
    all_to_all x1, starting transfers between devices, local(): lax.all_to_all(send_goal, 'mp', split_axis=0, concat_axis=0, tiled=True)  9.03 us
    gather x2, local copies, waits for them, and re-layouts, local(): jnp.take(combine, token_source, axis=0, mode='fill', fill_value=0)  8.52 us
    dot_general x1, matrix products, local(): lax.dot_general(piece, delta, (((0,), (0,)), ((), ())), preferred_element...  7.86 us
  transfers between devices with their start and end apart: 5, of which 5 were waited for; matrix products, arithmetic and copies ran while one was open for 14% of the time, Pallas kernels for 0%

commit v1 on v0

v1 whole, which is shorter than its diff:
```python
import functools

import jax
import jax.numpy as jnp
from jax import lax
from jax.experimental import pallas as pl
from jax.experimental.pallas import tpu as pltpu
from jax.sharding import PartitionSpec as P

MESH = pl.DeviceIdType.MESH
BF = jnp.bfloat16
F32 = jnp.float32
I32 = jnp.int32

W_CAP = 21
T_CAP = 42
STRIDE = 64
ROWS = 48
MAIN = 32
TAIL = 16
FOLD = 12
WINDOW = 2


def nn(a, b):
    return jnp.dot(a, b, preferred_element_type=F32)


def nt(a, b):
    return lax.dot_general(a, b, (((1,), (1,)), ((), ())), preferred_element_type=F32)


def tn(a, b):
    return lax.dot_general(a, b, (((0,), (0,)), ((), ())), preferred_element_type=F32)


def onehot(mask):
    return jnp.where(mask, 1.0, 0.0).astype(BF)


def iota(shape, axis):
    return lax.broadcasted_iota(I32, shape, axis)


def body(
    nx, nz, scale,
    gate_ref, up_ref, down_ref, part_ref, tok_ref, goal_ref, route_ref, comb_ref,
    out_ref,
    send_a, send_b, send_c, send_d, recv_a, recv_b, recv_c, recv_d,
    keyr, placer, xa, xb, qa, qc, wt, wd, wcol, grem, pbuf, sibrecv, ringp, ringm, hid, half,
    ssem, rsem, sib_s, sib_r, p_s, p_r, m_s, m_r, h_s, h_r, hs_s, hs_r,
):
    peers = nx * nz
    ny = hid.shape[1]
    chunks = peers // ny
    groups = ny // nx
    units = gate_ref.shape[0]
    cols = gate_ref.shape[1]
    count = tok_ref.shape[0]
    blocks = cols // 128
    folded = send_a.shape[1] - blocks * MAIN
    own_k = nx * (nz - 1)
    hp = ny // 2
    hm = ny - 1 - hp

    mp = lax.axis_index("mp")
    dp = lax.axis_index("dp")
    x, z = mp // nz, mp % nz
    y, c = dp // 2, dp % 2
    sibling = (y * 2 + 1 - c, mp)

    def shift(g):
        a = nz // 2 - 1 - g // 2
        odd = g % 2
        return (1 - odd) * (a + (nz // 2) * ((g + 2) // nz)) + odd * ((nz - a) % nz)

    def dest(g, dx):
        return ((x + dx) % nx) * nz + (z + shift(g)) % nz

    def source(k):
        g, dx = k // nx, k % nx
        return ((x + nx - dx) % nx) * nz + (z + nz - shift(g)) % nz

    def peer_y(dy):
        return ((y + ny + dy) % ny) * 2 + c

    barrier = pltpu.get_barrier_semaphore()

    def greet(k, carry):
        @pl.when(k != own_k)
        def _():
            pl.semaphore_signal(
                barrier, inc=1, device_id=(dp, dest(k // nx, k % nx)), device_id_type=MESH
            )

        return carry

    lax.fori_loop(0, peers, greet, 0)
    for dy in range(1, ny):
        pl.semaphore_signal(barrier, inc=1, device_id=(peer_y(dy), mp), device_id_type=MESH)
    pl.semaphore_signal(barrier, inc=1, device_id=sibling, device_id_type=MESH)

    tri_u = onehot(iota((units, units), 0) <= iota((units, units), 1))
    my_part = part_ref[pl.ds(mp, 1), :]
    my_owner = jnp.floor((my_part.astype(F32) + 0.5) * (1.0 / units)).astype(I32)
    hot = iota((peers, units), 0) == my_owner
    ahead = nn(onehot(hot), tri_u)
    rank = jnp.sum(ahead * jnp.where(hot, 1.0, 0.0), axis=0, keepdims=True) - 1.0
    unit_key = my_owner * STRIDE + rank.astype(I32)

    sends = (send_a, send_b, send_c, send_d)
    recvs = (recv_a, recv_b, recv_c, recv_d)

    def copy_k(kind, k):
        return pltpu.make_async_remote_copy(
            src_ref=sends[kind].at[k],
            dst_ref=recvs[kind].at[k],
            send_sem=ssem.at[kind, k],
            recv_sem=rsem.at[kind, k],
            device_id=(dp, dest(k // nx, k % nx)),
            device_id_type=MESH,
        )

    def chunk_loop(j, step):
        def run(k, carry):
            @pl.when(k != own_k)
            def _():
                step(k)

            return carry

        lax.fori_loop(j * ny, (j + 1) * ny, run, 0)

    def start(kind, j):
        if j < chunks:
            chunk_loop(j, lambda k: copy_k(kind, k).start())

    def sent(kind, j):
        chunk_loop(j, lambda k: copy_k(kind, k).wait_send())

    def arrive(kind, j):
        chunk_loop(j, lambda k: copy_k(kind, k).wait_recv())

    fold_rows = iota((folded, blocks * TAIL), 0)
    fold_cols = iota((folded, blocks * TAIL), 1)
    fold = onehot(
        (fold_cols % TAIL < FOLD) & (fold_rows == (fold_cols // TAIL) * FOLD + fold_cols % TAIL)
    )
    open_rows = iota((blocks * TAIL, folded), 0)
    open_cols = iota((blocks * TAIL, folded), 1)
    unfold = onehot(
        (open_rows % TAIL < FOLD) & (open_cols == (open_rows // TAIL) * FOLD + open_rows % TAIL)
    )

    def column(b):
        return slice(b * 128, (b + 1) * 128)

    def pack(block, send, g):
        tails = []
        for dx in range(nx):
            rows = block[dx * ROWS : (dx + 1) * ROWS]
            for b in range(blocks):
                send[g * nx + dx, b * MAIN : (b + 1) * MAIN, :] = rows[:MAIN, column(b)]
            tails.append(jnp.concatenate([rows[MAIN:, column(b)] for b in range(blocks)], axis=0))
        rest = nn(fold, jnp.concatenate(tails, axis=1)).astype(BF)
        for dx in range(nx):
            send[g * nx + dx, blocks * MAIN :, :] = rest[:, column(dx)]

    def unpack(recv, full, g):
        rest = jnp.concatenate([recv[g * nx + dx, blocks * MAIN :, :] for dx in range(nx)], axis=1)
        tails = nn(unfold, rest).astype(BF)
        for dx in range(nx):
            k = g * nx + dx
            for b in range(blocks):
                full[k, :MAIN, column(b)] = recv[k, b * MAIN : (b + 1) * MAIN, :]
                full[k, MAIN:, column(b)] = tails[b * TAIL : (b + 1) * TAIL, column(dx)]

    def pick_of(key, g, rows, add):
        parts = []
        for dx in range(nx):
            want = iota((rows, key.shape[1]), 0) + (dest(g, dx) * STRIDE + add)
            parts.append(onehot(key == want))
        return jnp.concatenate(parts, axis=0)

    def make_a(g, carry):
        block = nn(pick_of(unit_key, g, ROWS, 0), gate_ref[...])
        block += nn(pick_of(unit_key, g, ROWS, -W_CAP), up_ref[...])
        pack(block.astype(BF), send_a, g)
        return carry

    for j in range(chunks):
        lax.fori_loop(j * groups, (j + 1) * groups, make_a, 0)
        if j == 0:
            pl.semaphore_wait(barrier, peers - 1 + ny)
        start(0, j)

    tri_t = onehot(iota((128, 128), 0) <= iota((128, 128), 1))
    before = jnp.zeros((peers, 1), F32)
    keys = []
    for b in range(count // 128):
        chosen = route_ref[:, column(b)]
        hot = iota((peers, 128), 0) == chosen
        ahead = nn(onehot(hot), tri_t) + before
        rank = jnp.sum(ahead * jnp.where(hot, 1.0, 0.0), axis=0, keepdims=True) - 1.0
        keys.append(chosen * STRIDE + rank.astype(I32))
        before = ahead[:, 127:128]
    token_key = jnp.concatenate(keys, axis=1)

    comb_rows = comb_ref[...].astype(F32)
    comb = jnp.concatenate([comb_rows[b : b + 1] for b in range(count // 128)], axis=1)
    comb = jnp.broadcast_to(comb, (16, count)).astype(BF)

    def make_b(g, carry):
        pack(nn(pick_of(token_key, g, ROWS, 0), tok_ref[...]).astype(BF), send_b, g)
        return carry

    def make_cd(g, carry):
        main = nn(pick_of(token_key, g, MAIN, 0), goal_ref[...]).astype(BF)
        late = pick_of(token_key, g, MAIN, MAIN - W_CAP)
        low = iota(late.shape, 0) % MAIN >= W_CAP
        late = jnp.where(low, late.astype(F32), 0.0).astype(BF)
        block = nn(late, goal_ref[...]) + nn(pick_of(unit_key, g, MAIN, 0), down_ref[...])
        weights = nt(comb, pick_of(token_key, g, STRIDE, 0))
        for dx in range(nx):
            k = g * nx + dx
            rows = block[dx * MAIN : (dx + 1) * MAIN]
            lanes = weights[0:1, column(dx // 2)]
            first = jnp.where(iota((MAIN, 128), 0) == MAIN - 1, lanes, rows[:, :128])
            send_c[k, :, :128] = first.astype(BF)
            send_c[k, :, 128:] = rows[:, 128:].astype(BF)
            send_d[k] = main[dx * MAIN : (dx + 1) * MAIN]
        return carry

    lax.fori_loop(0, nz, make_b, 0)
    lax.fori_loop(0, nz, make_cd, 0)
    for send, recv in zip(sends, recvs):
        recv[own_k] = send[own_k]

    part = part_ref[...]
    owner = jnp.floor((part.astype(F32) + 0.5) * (1.0 / units)).astype(I32)
    mine = owner == mp
    ahead = nn(onehot(mine), tri_u)
    keyr[...] = jnp.where(mine, ahead.astype(I32) - 1, -1000)
    placer[...] = jnp.where(mine, part - owner * units + 1, 0).astype(F32)

    def landing(k, rows):
        s = source(k)
        row = iota((rows, 1), 0)
        second = (row >= W_CAP).astype(I32) if rows == ROWS else jnp.zeros((rows, 1), I32)
        match = keyr[pl.ds(s, 1), :] == row - second * W_CAP
        found = jnp.sum(jnp.where(match, placer[pl.ds(s, 1), :], 0.0), axis=1, keepdims=True)
        return jnp.where(found > 0.0, found.astype(I32) - 1 + second * units, -1)

    def place_a(k, carry):
        qa[k] = onehot(landing(k, ROWS) == iota((ROWS, 2 * units), 1))
        return carry

    def place_c(k, carry):
        qc[k] = onehot(landing(k, MAIN) == iota((MAIN, units), 1))
        return carry

    lax.fori_loop(0, peers, place_a, 0)
    lax.fori_loop(0, peers, place_c, 0)

    for j in range(chunks):
        sent(0, j)
        if j < WINDOW:
            start(1, j)
    for j in range(chunks):
        arrive(0, j)

    def open_a(g, carry):
        unpack(recv_a, xa, g)
        return carry

    lax.fori_loop(0, nz, open_a, 0)
    wt[...] = tn(
        xa[...].reshape(peers * ROWS, cols), qa[...].reshape(peers * ROWS, 2 * units)
    ).astype(BF)

    def on_owner(stage):
        def run(j):
            @pl.when(c == j % 2)
            def _():
                stage(j)

        return run

    def remote(src, dst, send, recv, target):
        return pltpu.make_async_remote_copy(
            src_ref=src, dst_ref=dst, send_sem=send, recv_sem=recv,
            device_id=target, device_id_type=MESH,
        )

    def sib_copy(j):
        return remote(pbuf.at[j], sibrecv.at[j // 2], sib_s.at[j], sib_r.at[j], sibling)

    def plus_copy(j, s):
        src = pbuf.at[j, (y + hp) % ny] if s == 0 else ringp.at[j // 2, s - 1]
        return remote(src, ringp.at[j // 2, s], p_s.at[j, s], p_r.at[j, s], (peer_y(1), mp))

    def minus_copy(j, s):
        src = pbuf.at[j, (y + ny - hm) % ny] if s == 0 else ringm.at[j // 2, s - 1]
        return remote(src, ringm.at[j // 2, s], m_s.at[j, s], m_r.at[j, s], (peer_y(-1), mp))

    def h_copy(j, dy):
        return remote(hid.at[j, y], hid.at[j, y], h_s.at[j, dy], h_r.at[j, dy], (peer_y(dy), mp))

    def h_arrival(j, dy):
        src = (y + ny - dy) % ny
        return remote(hid.at[j, src], hid.at[j, src], h_s.at[j, dy], h_r.at[j, dy], (peer_y(dy), mp))

    def hs_copy(j):
        return remote(hid.at[j], hid.at[j], hs_s.at[j], hs_r.at[j], sibling)

    def partial(j):
        arrive(1, j)

        def open_b(g, carry):
            unpack(recv_b, xb, g)
            return carry

        lax.fori_loop(j * groups, (j + 1) * groups, open_b, 0)
        rows = xb[j * ny : (j + 1) * ny].reshape(ny * ROWS, cols)
        pbuf[j] = nn(rows, wt[...]).reshape(ny, ROWS, 2 * units)

        @pl.when(c != j % 2)
        def _():
            sib_copy(j).start()

    @on_owner
    def ring_first(j):
        sib_copy(j).wait_recv()
        pbuf[j] += sibrecv[j // 2]
        plus_copy(j, 0).start()
        if hm > 0:
            minus_copy(j, 0).start()

    def ring_step(s):
        @on_owner
        def run(j):
            if s < hp:
                plus_copy(j, s - 1).wait_recv()
                ringp[j // 2, s - 1] += pbuf[j, (y + hp - s) % ny]
                plus_copy(j, s).start()
            if s < hm:
                minus_copy(j, s - 1).wait_recv()
                ringm[j // 2, s - 1] += pbuf[j, (y + ny - hm + s) % ny]
                minus_copy(j, s).start()

        return run

    @on_owner
    def combine(j):
        plus_copy(j, hp - 1).wait_recv()
        total = pbuf[j, y] + ringp[j // 2, hp - 1]
        if hm > 0:
            minus_copy(j, hm - 1).wait_recv()
            total += ringm[j // 2, hm - 1]
        gate = total[:, :units]
        value = gate / (1.0 + jnp.exp(-gate)) * total[:, units:]
        hid[j, y] = value.astype(BF)
        for dy in range(1, ny):
            h_copy(j, dy).start()

    @on_owner
    def share(j):
        for dy in range(1, ny):
            h_arrival(j, dy).wait_recv()
        hs_copy(j).start()

    pick_late = onehot(
        (iota((TAIL, MAIN), 1) == iota((TAIL, MAIN), 0) + W_CAP)
        & (iota((TAIL, MAIN), 0) < T_CAP - MAIN)
    )

    def open_c(j):
        arrive(2, j)

        def run(k, carry):
            grem[k] = nn(pick_late, recv_c[k]).astype(BF)
            last = recv_c[k, MAIN - 16 :, 0:128].astype(F32)[15:16]
            lane = iota((ROWS, 128), 1) - (k % nx % 2) * STRIDE
            eye = lane == iota((ROWS, 128), 0)
            wcol[k] = jnp.sum(jnp.where(eye, last, 0.0), axis=1, keepdims=True)
            return carry

        lax.fori_loop(j * ny, (j + 1) * ny, run, 0)

    def close_c():
        wd[...] = tn(
            qc[...].reshape(peers * MAIN, units), recv_c[...].reshape(peers * MAIN, cols)
        ).astype(BF)

    def student(j):
        @pl.when(c != j % 2)
        def _():
            hs_copy(j).wait_recv()

        weight = wcol[j * ny : (j + 1) * ny].reshape(ny * ROWS, 1)
        half[j] = weight * nn(hid[j].reshape(ny * ROWS, units), wd[...])

    def finish(j):
        arrive(3, j)
        goal = jnp.concatenate(
            [recv_d[j * ny : (j + 1) * ny], grem[j * ny : (j + 1) * ny]], axis=1
        ).reshape(ny * ROWS, cols)
        weight = wcol[j * ny : (j + 1) * ny].reshape(ny * ROWS, 1)
        delta = (weight * (half[j] - goal.astype(F32)) * scale).astype(BF)
        gradient = tn(hid[j].reshape(ny * ROWS, units), delta)
        if j == 0:
            out_ref[...] = gradient
        else:
            out_ref[...] += gradient

    ring_steps = [ring_step(s) for s in range(1, max(hp, hm))]
    stages = [partial, ring_first] + ring_steps + [combine, share]
    followers = {}

    def follow(kind, j, *starts):
        followers[len(followers)] = (kind, j, starts)

    for j in range(chunks):
        if j + WINDOW < chunks:
            follow(1, j, (1, j + WINDOW))
        elif j + 1 < chunks:
            follow(1, j, (2, 0), (2, 1))
        else:
            rest = [(2, i) for i in range(2 if chunks > 1 else 0, chunks)]
            follow(1, j, *rest, (3, 0))
    for j in range(chunks):
        follow(2, j, (3, j + 1))
    for t in range(max(chunks + len(stages) - 1, len(followers))):
        for at in reversed(range(1, len(stages))):
            if 0 <= t - at < chunks:
                stages[at](t - at)
        if t < chunks:
            partial(t)
        if t in followers:
            kind, j, starts = followers[t]
            sent(kind, j)
            for later in starts:
                start(*later)
    for j in range(chunks):
        open_c(j)
    close_c()
    for j in range(chunks):
        student(j)
    for j in range(chunks):
        finish(j)

    for j in range(chunks):
        sent(3, j)
    for j in range(chunks):
        @pl.when(c == j % 2)
        def _():
            for s in range(hp):
                plus_copy(j, s).wait_send()
            for s in range(hm):
                minus_copy(j, s).wait_send()
            for dy in range(1, ny):
                h_copy(j, dy).wait_send()
            hs_copy(j).wait_send()

        @pl.when(c != j % 2)
        def _():
            sib_copy(j).wait_send()


def build(mesh, nx, nz):
    peers = mesh.shape["mp"]
    ny = mesh.shape["dp"] // 2
    chunks = peers // ny
    slots = (chunks + 1) // 2
    hp = ny // 2
    hm = max(1, ny - 1 - hp)

    def local(gate_proj, up_proj, down_proj, partition, tokens, targets, routes, combine):
        units, cols = gate_proj.shape
        count = tokens.shape[0]
        blocks = cols // 128
        packed = blocks * MAIN + -(-blocks * FOLD // 16) * 16
        vmem = pl.BlockSpec(memory_space=pltpu.VMEM)
        dma = pltpu.SemaphoreType.DMA
        flops = 2 * peers * ROWS * units * cols * 4
        messages = [
            pltpu.VMEM((peers, packed, 128), BF),
            pltpu.VMEM((peers, packed, 128), BF),
            pltpu.VMEM((peers, MAIN, cols), BF),
            pltpu.VMEM((peers, MAIN, cols), BF),
        ]
        gradient = pl.pallas_call(
            functools.partial(body, nx, nz, count ** (-0.5)),
            out_shape=jax.ShapeDtypeStruct((units, cols), F32),
            in_specs=[vmem] * 8,
            out_specs=vmem,
            scratch_shapes=messages + messages + [
                pltpu.VMEM((peers, units), I32),
                pltpu.VMEM((peers, units), F32),
                pltpu.VMEM((peers, ROWS, cols), BF),
                pltpu.VMEM((peers, ROWS, cols), BF),
                pltpu.VMEM((peers, ROWS, 2 * units), BF),
                pltpu.VMEM((peers, MAIN, units), BF),
                pltpu.VMEM((cols, 2 * units), BF),
                pltpu.VMEM((units, cols), BF),
                pltpu.VMEM((peers, ROWS, 1), F32),
                pltpu.VMEM((peers, TAIL, cols), BF),
                pltpu.VMEM((chunks, ny, ROWS, 2 * units), F32),
                pltpu.VMEM((slots, ny, ROWS, 2 * units), F32),
                pltpu.VMEM((slots, hp, ROWS, 2 * units), F32),
                pltpu.VMEM((slots, hm, ROWS, 2 * units), F32),
                pltpu.VMEM((chunks, ny, ROWS, units), BF),
                pltpu.VMEM((chunks, ny * ROWS, cols), F32),
                dma((4, peers)),
                dma((4, peers)),
                dma((chunks,)),
                dma((chunks,)),
                dma((chunks, hp)),
                dma((chunks, hp)),
                dma((chunks, hm)),
                dma((chunks, hm)),
                dma((chunks, ny)),
                dma((chunks, ny)),
                dma((chunks,)),
                dma((chunks,)),
            ],
            compiler_params=pltpu.CompilerParams(
                collective_id=0, has_side_effects=True, vmem_limit_bytes=56 << 20
            ),
            cost_estimate=pl.CostEstimate(
                flops=flops, bytes_accessed=8 << 20, transcendentals=0
            ),
            name="distill",
        )(
            gate_proj,
            up_proj,
            down_proj.T,
            partition.reshape(peers, units),
            tokens,
            targets,
            routes.reshape(1, count),
            combine.reshape(count // 128, 128),
        )
        return gradient[None]

    in_specs = (
        P("mp", "dp"),
        P("mp", "dp"),
        P("dp", "mp"),
        P(),
        P("mp", "dp"),
        P("mp", "dp"),
        P("mp", None),
        P("mp"),
    )
    out_specs = P("mp", None, "dp")
    return jax.shard_map(local, mesh=mesh, in_specs=in_specs, out_specs=out_specs, check_vma=False)


def solution(mesh):
    return build(mesh, 4, mesh.shape["mp"] // 4)
```

time: 316 us -> 147 us (0.47)
  the two profiles are of different devices: /device:TPU:25 before, /device:TPU:150 now
where the time goes in v1:
time: 147 us
  Pallas kernels  143 us (97%)
  local copies, waits for them, and re-layouts  3.69 us (3%)
    pallas_call x1, Pallas kernels, local(): pl.pallas_call(functools.partial(body, nx, nz, count ** (-0.5)), out_shap...  143 us

profile of v1, /device:TPU:150, one launch (start us, length us, event | category | flops | bytes accessed | tf_op | source)
XLA Modules:
  0.0 147.1 jit_solution(15019147204128969918)
XLA Ops:
  0.0 1.5 %reshape.9.part_ref = s32[32,448]{1,0:T(8,128)} reshape(s32[14336]{0:T(1024)} %param.11) | data formatting | bytes 114688 | tf_op jit(solution)/shard_map/reshape | solution.py:538
  1.5 143.4 %distill.1 = f32[448,512]{1,0:T(8,128)} custom-call(bf16[448,512]{1,0:T(8,128)(2,1)} %gate_ref.1, bf16[448,512]{1,0:T(8,128)(2,1)} %up_ref.1, bf16[448,512]{1,0:T(8,128)(2,1)} %bitcast.5, s32[32,448]{1,0:T(8,128)} %reshape.9.part_ref, bf16[1024,512]{1,0:T(8,128)(2,1)} %tok_ref.1, bf16[1024,512]{1,0:T(8,128)(2,1)} %goal_ref.1, s32[1,1024]{1,0:T(1,128)} %bitcast.6, ...), custom_call_target="tpu_custom_call" | custom-call | flops 2818572288 | bytes 8388608 | tf_op jit(solution)/shard_map/distill/pallas_call | solution.py:492
  145.0 2.2 %copy.10 = f32[1,448,512]{2,1,0:T(8,128)} copy(f32[1,448,512]{2,1,0:T(8,128)} %bitcast.4) | data formatting | bytes 1835008

commit v2 on v1

--- a/solution.py
+++ b/solution.py
@@ -19,7 +19,7 @@
 MAIN = 32
 TAIL = 16
 FOLD = 12
-WINDOW = 2
+PIECES = 2
 
 
 def nn(a, b):
@@ -47,7 +47,7 @@
     gate_ref, up_ref, down_ref, part_ref, tok_ref, goal_ref, route_ref, comb_ref,
     out_ref,
     send_a, send_b, send_c, send_d, recv_a, recv_b, recv_c, recv_d,
-    keyr, placer, xa, xb, qa, qc, wt, wd, wcol, grem, pbuf, sibrecv, ringp, ringm, hid, half,
+    part_rows, keyr, placer, xa, xb, qa, qc, qt, wt, wd, wcol, turned, pbuf, sibrecv, ringp, ringm, hid, half,
     ssem, rsem, sib_s, sib_r, p_s, p_r, m_s, m_r, h_s, h_r, hs_s, hs_r,
 ):
     peers = nx * nz
@@ -101,7 +101,19 @@
     pl.semaphore_signal(barrier, inc=1, device_id=sibling, device_id_type=MESH)
 
     tri_u = onehot(iota((units, units), 0) <= iota((units, units), 1))
-    my_part = part_ref[pl.ds(mp, 1), :]
+    per = 2 * units // 128
+    if per * 128 == 2 * units:
+        wide = jnp.concatenate(
+            [part_ref[pl.ds(i, peers // 2, stride=per), :] for i in range(per)], axis=1
+        )
+        part_rows[...] = jnp.concatenate([wide[:, :units], wide[:, units:]], axis=0)
+    else:
+        part_rows[...] = jnp.concatenate([part_ref[h::2, :] for h in range(2)], axis=0)
+
+    def shard_row(s):
+        return (s % 2) * (peers // 2) + s // 2
+
+    my_part = part_rows[pl.ds(shard_row(mp), 1), :]
     my_owner = jnp.floor((my_part.astype(F32) + 0.5) * (1.0 / units)).astype(I32)
     hot = iota((peers, units), 0) == my_owner
     ahead = nn(onehot(hot), tri_u)
@@ -137,6 +149,24 @@
 
     def sent(kind, j):
         chunk_loop(j, lambda k: copy_k(kind, k).wait_send())
+
+    def swap(kind, j, *then):
+        def run(at, carry):
+            k = j * ny + at
+
+            @pl.when(k != own_k)
+            def _():
+                copy_k(kind, k).wait_send()
+
+            for later, i in then:
+
+                @pl.when(i * ny + at != own_k)
+                def _():
+                    copy_k(later, i * ny + at).start()
+
+            return carry
+
+        lax.fori_loop(0, ny, run, 0)
 
     def arrive(kind, j):
         chunk_loop(j, lambda k: copy_k(kind, k).wait_recv())
@@ -216,10 +246,8 @@
 
     def make_cd(g, carry):
         main = nn(pick_of(token_key, g, MAIN, 0), goal_ref[...]).astype(BF)
-        late = pick_of(token_key, g, MAIN, MAIN - W_CAP)
-        low = iota(late.shape, 0) % MAIN >= W_CAP
-        late = jnp.where(low, late.astype(F32), 0.0).astype(BF)
-        block = nn(late, goal_ref[...]) + nn(pick_of(unit_key, g, MAIN, 0), down_ref[...])
+        block = nn(pick_of(token_key, g, MAIN, MAIN), goal_ref[...])
+        block += nn(pick_of(unit_key, g, MAIN, MAIN - T_CAP), down_ref[...])
         weights = nt(comb, pick_of(token_key, g, STRIDE, 0))
         for dx in range(nx):
             k = g * nx + dx
@@ -236,36 +264,37 @@
     for send, recv in zip(sends, recvs):
         recv[own_k] = send[own_k]
 
-    part = part_ref[...]
+    part = part_rows[...]
     owner = jnp.floor((part.astype(F32) + 0.5) * (1.0 / units)).astype(I32)
     mine = owner == mp
     ahead = nn(onehot(mine), tri_u)
     keyr[...] = jnp.where(mine, ahead.astype(I32) - 1, -1000)
     placer[...] = jnp.where(mine, part - owner * units + 1, 0).astype(F32)
 
-    def landing(k, rows):
-        s = source(k)
-        row = iota((rows, 1), 0)
-        second = (row >= W_CAP).astype(I32) if rows == ROWS else jnp.zeros((rows, 1), I32)
-        match = keyr[pl.ds(s, 1), :] == row - second * W_CAP
+    def landing(k, rank, second):
+        s = shard_row(source(k))
+        match = keyr[pl.ds(s, 1), :] == rank
         found = jnp.sum(jnp.where(match, placer[pl.ds(s, 1), :], 0.0), axis=1, keepdims=True)
-        return jnp.where(found > 0.0, found.astype(I32) - 1 + second * units, -1)
+        return jnp.where(found > 0.0, found.astype(I32) - 1 + second, -1)
 
     def place_a(k, carry):
-        qa[k] = onehot(landing(k, ROWS) == iota((ROWS, 2 * units), 1))
+        row = iota((ROWS, 1), 0)
+        second = (row >= W_CAP).astype(I32)
+        target = landing(k, row - second * W_CAP, second * units)
+        qa[k] = onehot(target == iota((ROWS, 2 * units), 1))
         return carry
 
     def place_c(k, carry):
-        qc[k] = onehot(landing(k, MAIN) == iota((MAIN, units), 1))
+        row = iota((MAIN, 1), 0) - (T_CAP - MAIN)
+        qc[k] = onehot(landing(k, row, 0) == iota((MAIN, units), 1))
         return carry
 
     lax.fori_loop(0, peers, place_a, 0)
     lax.fori_loop(0, peers, place_c, 0)
+    qt[...] = qc[...].reshape(peers * MAIN, units).T
 
     for j in range(chunks):
-        sent(0, j)
-        if j < WINDOW:
-            start(1, j)
+        swap(0, j, *[(1, j)] * (j < 1))
     for j in range(chunks):
         arrive(0, j)
 
@@ -277,6 +306,9 @@
     wt[...] = tn(
         xa[...].reshape(peers * ROWS, cols), qa[...].reshape(peers * ROWS, 2 * units)
     ).astype(BF)
+
+    if chunks > 1:
+        start(1, 1)
 
     def on_owner(stage):
         def run(j):
@@ -292,19 +324,50 @@
             device_id=target, device_id_type=MESH,
         )
 
-    def sib_copy(j):
-        return remote(pbuf.at[j], sibrecv.at[j // 2], sib_s.at[j], sib_r.at[j], sibling)
-
-    def plus_copy(j, s):
-        src = pbuf.at[j, (y + hp) % ny] if s == 0 else ringp.at[j // 2, s - 1]
-        return remote(src, ringp.at[j // 2, s], p_s.at[j, s], p_r.at[j, s], (peer_y(1), mp))
-
-    def minus_copy(j, s):
-        src = pbuf.at[j, (y + ny - hm) % ny] if s == 0 else ringm.at[j // 2, s - 1]
-        return remote(src, ringm.at[j // 2, s], m_s.at[j, s], m_r.at[j, s], (peer_y(-1), mp))
+    order = []
+    for s in range(hp):
+        order.append(hp - s)
+        if s < hm:
+            order.append(s - hm)
+    order.append(0)
+
+    def sib_copy(j, offset):
+        at, block = order.index(offset), (y + ny + offset) % ny
+        return remote(
+            pbuf.at[j, block], sibrecv.at[j // 2, block], sib_s.at[j, at], sib_r.at[j, at], sibling
+        )
+
+    def joined(j, offset):
+        sib_copy(j, offset).wait_recv()
+        block = (y + ny + offset) % ny
+        return pbuf[j, block] + sibrecv[j // 2, block]
+
+    piece = ROWS // PIECES
+
+    def cut(h):
+        return pl.ds(h * piece, piece)
+
+    def plus_copy(j, s, h):
+        if s == 0:
+            src = pbuf.at[j, (y + hp) % ny, cut(h)]
+        else:
+            src = ringp.at[j // 2, s - 1, cut(h)]
+        dst = ringp.at[j // 2, s, cut(h)]
+        return remote(src, dst, p_s.at[j, s, h], p_r.at[j, s, h], (peer_y(1), mp))
+
+    def minus_copy(j, s, h):
+        if s == 0:
+            src = pbuf.at[j, (y + ny - hm) % ny, cut(h)]
+        else:
+            src = ringm.at[j // 2, s - 1, cut(h)]
+        dst = ringm.at[j // 2, s, cut(h)]
+        return remote(src, dst, m_s.at[j, s, h], m_r.at[j, s, h], (peer_y(-1), mp))
+
+    far = hp if hp > 1 else 0
 
     def h_copy(j, dy):
-        return remote(hid.at[j, y], hid.at[j, y], h_s.at[j, dy], h_r.at[j, dy], (peer_y(dy), mp))
+        at, to = (y, dy) if dy != far else ((y + ny - far + 1) % ny, 1)
+        return remote(hid.at[j, at], hid.at[j, at], h_s.at[j, dy], h_r.at[j, dy], (peer_y(to), mp))
 
     def h_arrival(j, dy):
         src = (y + ny - dy) % ny
@@ -326,59 +389,71 @@
 
         @pl.when(c != j % 2)
         def _():
-            sib_copy(j).start()
+            for offset in order:
+                sib_copy(j, offset).start()
 
     @on_owner
     def ring_first(j):
-        sib_copy(j).wait_recv()
-        pbuf[j] += sibrecv[j // 2]
-        plus_copy(j, 0).start()
+        pbuf[j, (y + hp) % ny] = joined(j, hp)
+        for h in range(PIECES):
+            plus_copy(j, 0, h).start()
         if hm > 0:
-            minus_copy(j, 0).start()
+            pbuf[j, (y + ny - hm) % ny] = joined(j, -hm)
+            for h in range(PIECES):
+                minus_copy(j, 0, h).start()
 
     def ring_step(s):
         @on_owner
         def run(j):
             if s < hp:
-                plus_copy(j, s - 1).wait_recv()
-                ringp[j // 2, s - 1] += pbuf[j, (y + hp - s) % ny]
-                plus_copy(j, s).start()
+                block_p = (y + hp - s) % ny
+                pbuf[j, block_p] = joined(j, hp - s)
             if s < hm:
-                minus_copy(j, s - 1).wait_recv()
-                ringm[j // 2, s - 1] += pbuf[j, (y + ny - hm + s) % ny]
-                minus_copy(j, s).start()
+                block_m = (y + ny - hm + s) % ny
+                pbuf[j, block_m] = joined(j, s - hm)
+            for h in range(PIECES):
+                if s < hp:
+                    plus_copy(j, s - 1, h).wait_recv()
+                    ringp[j // 2, s - 1, cut(h)] += pbuf[j, block_p, cut(h)]
+                    plus_copy(j, s, h).start()
+                if s < hm:
+                    minus_copy(j, s - 1, h).wait_recv()
+                    ringm[j // 2, s - 1, cut(h)] += pbuf[j, block_m, cut(h)]
+                    minus_copy(j, s, h).start()
 
         return run
 
     @on_owner
     def combine(j):
-        plus_copy(j, hp - 1).wait_recv()
-        total = pbuf[j, y] + ringp[j // 2, hp - 1]
+        total = joined(j, 0)
+        for h in range(PIECES):
+            plus_copy(j, hp - 1, h).wait_recv()
+            if hm > 0:
+                minus_copy(j, hm - 1, h).wait_recv()
+        total += ringp[j // 2, hp - 1]
         if hm > 0:
-            minus_copy(j, hm - 1).wait_recv()
             total += ringm[j // 2, hm - 1]
         gate = total[:, :units]
         value = gate / (1.0 + jnp.exp(-gate)) * total[:, units:]
         hid[j, y] = value.astype(BF)
         for dy in range(1, ny):
-            h_copy(j, dy).start()
+            if dy != far:
+                h_copy(j, dy).start()
 
     @on_owner
     def share(j):
+        if far:
+            h_arrival(j, far - 1).wait_recv()
+            h_copy(j, far).start()
         for dy in range(1, ny):
-            h_arrival(j, dy).wait_recv()
+            if dy != far - 1:
+                h_arrival(j, dy).wait_recv()
         hs_copy(j).start()
-
-    pick_late = onehot(
-        (iota((TAIL, MAIN), 1) == iota((TAIL, MAIN), 0) + W_CAP)
-        & (iota((TAIL, MAIN), 0) < T_CAP - MAIN)
-    )
 
     def open_c(j):
         arrive(2, j)
 
         def run(k, carry):
-            grem[k] = nn(pick_late, recv_c[k]).astype(BF)
             last = recv_c[k, MAIN - 16 :, 0:128].astype(F32)[15:16]
             lane = iota((ROWS, 128), 1) - (k % nx % 2) * STRIDE
             eye = lane == iota((ROWS, 128), 0)
@@ -388,9 +463,7 @@
         lax.fori_loop(j * ny, (j + 1) * ny, run, 0)
 
     def close_c():
-        wd[...] = tn(
-            qc[...].reshape(peers * MAIN, units), recv_c[...].reshape(peers * MAIN, cols)
-        ).astype(BF)
+        wd[...] = nn(qt[...], recv_c[...].reshape(peers * MAIN, cols)).astype(BF)
 
     def student(j):
         @pl.when(c != j % 2)
@@ -398,73 +471,77 @@
             hs_copy(j).wait_recv()
 
         weight = wcol[j * ny : (j + 1) * ny].reshape(ny * ROWS, 1)
-        half[j] = weight * nn(hid[j].reshape(ny * ROWS, units), wd[...])
+        hidden = hid[j].reshape(ny * ROWS, units)
+        half[j] = weight * nn(hidden, wd[...])
+        turned[j] = hidden.T
 
     def finish(j):
         arrive(3, j)
         goal = jnp.concatenate(
-            [recv_d[j * ny : (j + 1) * ny], grem[j * ny : (j + 1) * ny]], axis=1
+            [recv_d[j * ny : (j + 1) * ny], recv_c[j * ny : (j + 1) * ny, :TAIL]], axis=1
         ).reshape(ny * ROWS, cols)
         weight = wcol[j * ny : (j + 1) * ny].reshape(ny * ROWS, 1)
         delta = (weight * (half[j] - goal.astype(F32)) * scale).astype(BF)
-        gradient = tn(hid[j].reshape(ny * ROWS, units), delta)
+        gradient = nn(turned[j], delta)
         if j == 0:
             out_ref[...] = gradient
         else:
             out_ref[...] += gradient
 
     ring_steps = [ring_step(s) for s in range(1, max(hp, hm))]
-    stages = [partial, ring_first] + ring_steps + [combine, share]
-    followers = {}
-
-    def follow(kind, j, *starts):
-        followers[len(followers)] = (kind, j, starts)
-
-    for j in range(chunks):
-        if j + WINDOW < chunks:
-            follow(1, j, (1, j + WINDOW))
-        elif j + 1 < chunks:
-            follow(1, j, (2, 0), (2, 1))
-        else:
-            rest = [(2, i) for i in range(2 if chunks > 1 else 0, chunks)]
-            follow(1, j, *rest, (3, 0))
-    for j in range(chunks):
-        follow(2, j, (3, j + 1))
-    for t in range(max(chunks + len(stages) - 1, len(followers))):
-        for at in reversed(range(1, len(stages))):
-            if 0 <= t - at < chunks:
-                stages[at](t - at)
-        if t < chunks:
-            partial(t)
-        if t in followers:
-            kind, j, starts = followers[t]
-            sent(kind, j)
-            for later in starts:
-                start(*later)
+    queue = [(kind, j) for kind in (1, 2, 3) for j in range(chunks)]
+    queue = queue[2 if chunks > 1 else 1 :]
+    pace = (1, 1, 2, 3, 2, 1)
+
+    def at(stages, j):
+        if 0 <= j < chunks:
+            for stage in stages:
+                stage(j)
+
+    for t in range(chunks + 2):
+        at([partial], t)
+        for _ in range(pace[min(t, len(pace) - 1)]):
+            if queue:
+                start(*queue.pop(0))
+        at([ring_first], t)
+        at([combine], t - 2)
+        at([share], t - 3)
+        at(ring_steps[1:2], t - 1)
+        at(ring_steps[:1], t)
+        at(ring_steps[2:], t - 1)
+    while queue:
+        start(*queue.pop(0))
     for j in range(chunks):
         open_c(j)
     close_c()
+    at([share], chunks - 1)
+    for j in range(max(1, chunks - 1)):
+        student(j)
+    finish(0)
+    if chunks > 1:
+        student(chunks - 1)
+    for j in range(1, chunks):
+        finish(j)
+
     for j in range(chunks):
-        student(j)
-    for j in range(chunks):
-        finish(j)
-
-    for j in range(chunks):
-        sent(3, j)
+        for kind in (1, 2, 3):
+            sent(kind, j)
     for j in range(chunks):
         @pl.when(c == j % 2)
         def _():
-            for s in range(hp):
-                plus_copy(j, s).wait_send()
-            for s in range(hm):
-                minus_copy(j, s).wait_send()
+            for h in range(PIECES):
+                for s in range(hp):
+                    plus_copy(j, s, h).wait_send()
+                for s in range(hm):
+                    minus_copy(j, s, h).wait_send()
             for dy in range(1, ny):
                 h_copy(j, dy).wait_send()
             hs_copy(j).wait_send()
 
         @pl.when(c != j % 2)
         def _():
-            sib_copy(j).wait_send()
+            for offset in order:
+                sib_copy(j, offset).wait_send()
 
 
 def build(mesh, nx, nz):
@@ -480,6 +557,8 @@
         count = tokens.shape[0]
         blocks = cols // 128
         packed = blocks * MAIN + -(-blocks * FOLD // 16) * 16
+        whole = 2 * units % 128 == 0
+        part_shape = (partition.size // 128, 128) if whole else (peers, units)
         vmem = pl.BlockSpec(memory_space=pltpu.VMEM)
         dma = pltpu.SemaphoreType.DMA
         flops = 2 * peers * ROWS * units * cols * 4
@@ -496,15 +575,17 @@
             out_specs=vmem,
             scratch_shapes=messages + messages + [
                 pltpu.VMEM((peers, units), I32),
+                pltpu.VMEM((peers, units), I32),
                 pltpu.VMEM((peers, units), F32),
                 pltpu.VMEM((peers, ROWS, cols), BF),
                 pltpu.VMEM((peers, ROWS, cols), BF),
                 pltpu.VMEM((peers, ROWS, 2 * units), BF),
                 pltpu.VMEM((peers, MAIN, units), BF),
+                pltpu.VMEM((units, peers * MAIN), BF),
                 pltpu.VMEM((cols, 2 * units), BF),
                 pltpu.VMEM((units, cols), BF),
                 pltpu.VMEM((peers, ROWS, 1), F32),
-                pltpu.VMEM((peers, TAIL, cols), BF),
+                pltpu.VMEM((chunks, units, ny * ROWS), BF),
                 pltpu.VMEM((chunks, ny, ROWS, 2 * units), F32),
                 pltpu.VMEM((slots, ny, ROWS, 2 * units), F32),
                 pltpu.VMEM((slots, hp, ROWS, 2 * units), F32),
@@ -513,12 +594,12 @@
                 pltpu.VMEM((chunks, ny * ROWS, cols), F32),
                 dma((4, peers)),
                 dma((4, peers)),
-                dma((chunks,)),
-                dma((chunks,)),
-                dma((chunks, hp)),
-                dma((chunks, hp)),
-                dma((chunks, hm)),
-                dma((chunks, hm)),
+                dma((chunks, ny)),
+                dma((chunks, ny)),
+                dma((chunks, hp, PIECES)),
+                dma((chunks, hp, PIECES)),
+                dma((chunks, hm, PIECES)),
+                dma((chunks, hm, PIECES)),
                 dma((chunks, ny)),
                 dma((chunks, ny)),
                 dma((chunks,)),
@@ -535,7 +616,7 @@
             gate_proj,
             up_proj,
             down_proj.T,
-            partition.reshape(peers, units),
+            partition.reshape(part_shape),
             tokens,
             targets,
             routes.reshape(1, count),

time: 147 us -> 139 us (0.946)
  the two profiles are of different devices: /device:TPU:150 before, /device:TPU:64 now
where the time goes in v2:
time: 139 us; the launch traced here: 138 us
  Pallas kernels  136 us (98%)
  local copies, waits for them, and re-layouts  2.16 us (2%)
    pallas_call x1, Pallas kernels, local(): pl.pallas_call(functools.partial(body, nx, nz, count ** (-0.5)), out_shap...  136 us

profile of v2, /device:TPU:64, one launch (start us, length us, event | category | flops | bytes accessed | tf_op | source)
XLA Modules:
  0.0 138.3 jit_solution(10898193085234363019)
XLA Ops:
  0.0 136.1 %distill.1 = f32[448,512]{1,0:T(8,128)} custom-call(bf16[448,512]{1,0:T(8,128)(2,1)} %gate_ref.1, bf16[448,512]{1,0:T(8,128)(2,1)} %up_ref.1, bf16[448,512]{1,0:T(8,128)(2,1)} %bitcast.6, s32[112,128]{1,0:T(8,128)} %bitcast.7, bf16[1024,512]{1,0:T(8,128)(2,1)} %tok_ref.1, bf16[1024,512]{1,0:T(8,128)(2,1)} %goal_ref.1, s32[1,1024]{1,0:T(1,128)} %bitcast.8, ...), custom_call_target="tpu_custom_call" | custom-call | flops 2818572288 | bytes 8388608 | tf_op jit(solution)/shard_map/distill/pallas_call | solution.py:571
  136.1 2.2 %copy.10 = f32[1,448,512]{2,1,0:T(8,128)} copy(f32[1,448,512]{2,1,0:T(8,128)} %bitcast.5) | data formatting | bytes 1835008

commit v3 on v2

--- a/solution.py
+++ b/solution.py
@@ -44,8 +44,8 @@
 
 def body(
     nx, nz, scale,
-    gate_ref, up_ref, down_ref, part_ref, tok_ref, goal_ref, route_ref, comb_ref,
-    out_ref,
+    gate_ref, up_ref, down_hbm, part_ref, tok_hbm, goal_hbm, route_ref, comb_ref,
+    out_ref, down_ref, tok_ref, goal_ref, load_sem,
     send_a, send_b, send_c, send_d, recv_a, recv_b, recv_c, recv_d,
     part_rows, keyr, placer, xa, xb, qa, qc, qt, wt, wd, wcol, turned, pbuf, sibrecv, ringp, ringm, hid, half,
     ssem, rsem, sib_s, sib_r, p_s, p_r, m_s, m_r, h_s, h_r, hs_s, hs_r,
@@ -57,6 +57,14 @@
     units = gate_ref.shape[0]
     cols = gate_ref.shape[1]
     count = tok_ref.shape[0]
+    loads = [
+        pltpu.make_async_copy(src, dst, load_sem.at[i])
+        for i, (src, dst) in enumerate(
+            ((tok_hbm, tok_ref), (goal_hbm, goal_ref), (down_hbm, down_ref))
+        )
+    ]
+    for load in loads:
+        load.start()
     blocks = cols // 128
     folded = send_a.shape[1] - blocks * MAIN
     own_k = nx * (nz - 1)
@@ -259,7 +267,10 @@
             send_d[k] = main[dx * MAIN : (dx + 1) * MAIN]
         return carry
 
+    loads[0].wait()
     lax.fori_loop(0, nz, make_b, 0)
+    loads[1].wait()
+    loads[2].wait()
     lax.fori_loop(0, nz, make_cd, 0)
     for send, recv in zip(sends, recvs):
         recv[own_k] = send[own_k]
@@ -491,7 +502,7 @@
     ring_steps = [ring_step(s) for s in range(1, max(hp, hm))]
     queue = [(kind, j) for kind in (1, 2, 3) for j in range(chunks)]
     queue = queue[2 if chunks > 1 else 1 :]
-    pace = (1, 1, 2, 3, 2, 1)
+    pace = (1, 1, 2, 3, 1, 0)
 
     def at(stages, j):
         if 0 <= j < chunks:
@@ -509,22 +520,25 @@
         at(ring_steps[1:2], t - 1)
         at(ring_steps[:1], t)
         at(ring_steps[2:], t - 1)
+    for j in range(chunks):
+        swap(2, j, *queue[:1])
+        del queue[:1]
+        open_c(j)
     while queue:
         start(*queue.pop(0))
+    close_c()
+    for j in range(chunks - 2):
+        student(j)
+    at([share], chunks - 1)
+    for j in range(max(0, chunks - 2), chunks):
+        student(j)
+        if j >= 2:
+            finish(j - 2)
+    for j in range(max(0, chunks - 2), chunks):
+        finish(j)
+
     for j in range(chunks):
-        open_c(j)
-    close_c()
-    at([share], chunks - 1)
-    for j in range(max(1, chunks - 1)):
-        student(j)
-    finish(0)
-    if chunks > 1:
-        student(chunks - 1)
-    for j in range(1, chunks):
-        finish(j)
-
-    for j in range(chunks):
-        for kind in (1, 2, 3):
+        for kind in (1, 3):
             sent(kind, j)
     for j in range(chunks):
         @pl.when(c == j % 2)
@@ -560,6 +574,7 @@
         whole = 2 * units % 128 == 0
         part_shape = (partition.size // 128, 128) if whole else (peers, units)
         vmem = pl.BlockSpec(memory_space=pltpu.VMEM)
+        hbm = pl.BlockSpec(memory_space=pl.ANY)
         dma = pltpu.SemaphoreType.DMA
         flops = 2 * peers * ROWS * units * cols * 4
         messages = [
@@ -571,9 +586,14 @@
         gradient = pl.pallas_call(
             functools.partial(body, nx, nz, count ** (-0.5)),
             out_shape=jax.ShapeDtypeStruct((units, cols), F32),
-            in_specs=[vmem] * 8,
+            in_specs=[vmem, vmem, hbm, vmem, hbm, hbm, vmem, vmem],
             out_specs=vmem,
-            scratch_shapes=messages + messages + [
+            scratch_shapes=[
+                pltpu.VMEM((units, cols), BF),
+                pltpu.VMEM((count, cols), BF),
+                pltpu.VMEM((count, cols), BF),
+                dma((3,)),
+            ] + messages + messages + [
                 pltpu.VMEM((peers, units), I32),
                 pltpu.VMEM((peers, units), I32),
                 pltpu.VMEM((peers, units), F32),

time: 139 us -> 138 us (level)
  no operation moved by 1% of the time
where the time goes in v3:
time: 138 us
  Pallas kernels  136 us (99%)
  local copies, waits for them, and re-layouts  2.16 us (2%)
    pallas_call x1, Pallas kernels, local(): pl.pallas_call(functools.partial(body, nx, nz, count ** (-0.5)), out_shap...  136 us

profile of v3, /device:TPU:64, one launch (start us, length us, event | category | flops | bytes accessed | tf_op | source)
XLA Modules:
  0.0 138.0 jit_solution(12887828382943716013)
XLA Ops:
  0.0 135.9 %distill.1 = f32[448,512]{1,0:T(8,128)} custom-call(bf16[448,512]{1,0:T(8,128)(2,1)} %gate_ref.1, bf16[448,512]{1,0:T(8,128)(2,1)} %up_ref.1, bf16[448,512]{1,0:T(8,128)(2,1)} %bitcast.6, s32[112,128]{1,0:T(8,128)} %bitcast.7, bf16[1024,512]{1,0:T(8,128)(2,1)} %tok_hbm.1, bf16[1024,512]{1,0:T(8,128)(2,1)} %goal_hbm.1, s32[1,1024]{1,0:T(1,128)} %bitcast.8, ...), custom_call_target="tpu_custom_call" | custom-call | flops 2818572288 | bytes 8388608 | tf_op jit(solution)/shard_map/distill/pallas_call | solution.py:586
  135.9 2.2 %copy.10 = f32[1,448,512]{2,1,0:T(8,128)} copy(f32[1,448,512]{2,1,0:T(8,128)} %bitcast.5) | data formatting | bytes 1835008
